TPU v7x, 128 devices: a whole 4x4x4 slice. The times are simulated.
128 devices in a mesh: own: 16 (over x, z), help: 8 (over y, core).
Axes of the slice: x: 4, y: 4, z: 4, core: 2. Of those that a mesh axis runs over, the one named last changes fastest.
Arguments:
- points: bfloat16 [524288, 1024], P(('own', 'help')), may hold values from -64 to 64
- cluster_of: int32 [524288, 1], P(('own', 'help')), may hold values from 0 to 63; in each aligned block of 4096 rows (0 to 4095, 4096 to 8191, ...) at most 80 rows name the same one
- sub_init: int32 [524288], P(('own', 'help')), may hold values from 0 to 63
Outputs:
- centroids: float32 [64, 64, 1024], P(None, 'own')
Inputs may be any that keep to these rules, and one draw needn't show every extreme that they name: `cluster_of`: among the 4096 rows of one device no cluster appears more than 80 times; some cluster appears exactly 80 times in some device's rows.
All inputs are finite; a program needn't handle non-finite values.
Results may differ from a plain program's by a relative error of at most 0.04.
The roundings to bfloat16 on the way count: a program that leaves them out, or rounds other values in their place, can miss the bound.
Values may be sent and summed in bfloat16 or wider, within the bound.
A program may use at most 128 MiB of HBM per device.

v0:
```python
import jax
import jax.numpy as jnp
from jax import lax
from jax.sharding import PartitionSpec as P

SUB = 64
ITERS = 3
CL_DEV = 4


softness_level = 8.0


def partial_weight_sums(block, labels):
    onehot = (labels[..., None] == (jnp.arange(SUB) + 1).astype(jnp.bfloat16)).astype(jnp.bfloat16)
    sums = jnp.einsum("oqmk,oqmd->kqd", onehot, block, preferred_element_type=jnp.float32)
    mass = jnp.einsum("oqmk->kq", onehot.astype(jnp.float32))
    return (sums, mass)


def combine_help(sums, mass):
    total, weight = lax.psum((sums, mass), "help")
    return total / (weight[..., None] + 1.0)


def shards(points, cluster_of, sub_init):
    rows, width = points.shape
    owners = lax.axis_size("own")
    clusters = CL_DEV * owners
    most = rows // clusters + rows // (4 * clusters)
    label = cluster_of[:, 0]
    member = (label[:, None] == jnp.arange(clusters)[None, :]).astype(jnp.int32)
    rank = jnp.sum(jnp.cumsum(member, axis=0) * member, axis=1) - 1
    slot = label * most + rank
    outgoing = jnp.zeros((clusters * most, width), jnp.bfloat16).at[slot].set(points)
    tagged = (
        jnp.zeros((clusters * most,), jnp.bfloat16)
        .at[slot]
        .set((sub_init + 1).astype(jnp.bfloat16))
    )
    outgoing = outgoing.reshape(owners, CL_DEV, most, width)
    tagged = tagged.reshape(owners, CL_DEV, most)
    block, labels = (
        lax.all_to_all(outgoing, "own", split_axis=0, concat_axis=0, tiled=True),
        lax.all_to_all(tagged, "own", split_axis=0, concat_axis=0, tiled=True),
    )
    sums, mass = partial_weight_sums(block, labels)
    live = (labels > 0).astype(jnp.float32)
    current = combine_help(sums, mass)
    for turn in range(ITERS):
        current16 = current.astype(jnp.bfloat16)
        squared_norm_values = jnp.sum(current * current, axis=2)
        center_products = jnp.einsum(
            "oqmd,kqd->oqmk", block, current16, preferred_element_type=jnp.float32
        )
        distance_score = (
            2.0 * center_products - squared_norm_values.T[None, :, None, :]
        ) / softness_level
        weights = (jax.nn.softmax(distance_score, axis=-1) * live[..., None]).astype(jnp.bfloat16)
        sums = jnp.einsum("oqmk,oqmd->kqd", weights, block, preferred_element_type=jnp.float32)
        mass = jnp.einsum("oqmk->kq", weights.astype(jnp.float32))
        current = combine_help(sums, mass)
    return current


def solution(mesh):
    in_specs = (P(("own", "help"), None), P(("own", "help"), None), P(("own", "help")))
    out_specs = P(None, "own", None)
    return jax.shard_map(shards, mesh=mesh, in_specs=in_specs, out_specs=out_specs, check_vma=False)
```

profile of v0, /device:TPU:33, one launch (start us, length us, event | category | flops | bytes accessed | tf_op | source)
XLA Modules:
  0.0 598.9 jit_solution(17418271380314116538)
XLA Ops:
  7.4 18.4 %reduce-window.6 = s32[64,32,128]{2,1,0:T(8,128)S(1)} reduce-window(s32[64,32,128]{2,1,0:T(8,128)S(1)} %fusion.45, s32[]{:T(128)} %constant.13.clone.1), window={size=1x1x128 pad=0_0x0_0x127_0}, to_apply=%region_0.0 | reduce-window | flops 33292288 | bytes 2097156 | tf_op jit(solution)/shard_map/reduce-window
  28.1 28.6 %scatter_custom_fusion.1 = bf16[5120]{0:T(1024)(128)(2,1)S(1)} fusion(s32[4096]{0:T(1024)S(1)} %bitcast.109, bf16[4096]{0:T(1024)(128)(2,1)S(1)} %add_convert_fusion, bf16[]{:T(256)} %constant.11.clone.1), kind=kCustom, calls=%fused_computation.81 | custom fusion | bytes 10242 | tf_op jit(solution)/shard_map/scatter | solution.py:39
  57.3 7.3 %all-to-all-start.1 = ((bf16[16,4,80]{2,1,0:T(4,128)(2,1)}), bf16[16,4,80]{2,1,0:T(4,128)(2,1)S(1)}, u32[]{:S(2)}, u32[]{:S(2)}) async-start(bf16[16,4,80]{2,1,0:T(4,128)(2,1)} %reshape.57), calls=%async_computation.1 | async-start | bytes 32768 | tf_op jit(solution)/shard_map/all_to_all | solution.py:45
  64.7 25.3 %scatter_custom_fusion = bf16[5120,1024]{1,0:T(8,128)(2,1)} fusion(s32[4096]{0:T(1024)S(1)} %bitcast.110, bf16[4096,1024]{1,0:T(8,128)(2,1)} %param.3, bf16[]{:T(256)} %constant.11.clone.1), kind=kCustom, calls=%fused_computation.14 | custom fusion | bytes 10486272 | tf_op jit(solution)/shard_map/scatter | solution.py:35
  90.0 6.7 %all-to-all-start = ((bf16[16,4,80,1024]{3,2,1,0:T(8,128)(2,1)}), bf16[16,4,80,1024]{3,2,1,0:T(8,128)(2,1)}, u32[]{:S(2)}, u32[]{:S(2)}) async-start(bf16[16,4,80,1024]{3,2,1,0:T(8,128)(2,1)} %bitcast.102), calls=%async_computation | async-start | bytes 20971520 | tf_op jit(solution)/shard_map/all_to_all | solution.py:44
  96.7 175.8 %all-to-all-done = bf16[16,4,80,1024]{3,2,1,0:T(8,128)(2,1)} async-done(((bf16[16,4,80,1024]{3,2,1,0:T(8,128)(2,1)}), bf16[16,4,80,1024]{3,2,1,0:T(8,128)(2,1)}, u32[]{:S(2)}, u32[]{:S(2)}) %all-to-all-start) | async-done | bytes 10485792 | tf_op jit(solution)/shard_map/all_to_all | solution.py:44
  272.5 7.0 %fusion.28 = f32[64,4,1024]{2,0,1:T(8,128)} fusion(bf16[16,4,80,1024]{3,2,1,0:T(8,128)(2,1)} %all-to-all-done, bf16[16,4,80]{2,0,1:T(8,128)(2,1)S(1)} %copy.13, bf16[64]{0:T(256)(128)(2,1)S(1)} %add_convert_fusion.1), kind=kOutput, calls=%fused_computation.43 | convolution fusion | flops 671416320 | bytes 11544704 | tf_op jit(solution)/shard_map/oqmk,oqmd->kqd/dot_general | solution.py:16
  280.1 16.0 %psum.57 = f32[64,4]{0,1:T(4,128)S(1)} all-reduce(f32[64,4]{0,1:T(4,128)S(1)} %bitcast.111), channel_id=1, replica_groups=mesh['own'=16,'help'=8] {'help'}, use_global_device_ids=true, to_apply=%region_7.8 | all-reduce | flops 256 | bytes 2048 | tf_op jit(solution)/shard_map/psum | solution.py:22
  296.1 56.0 %all-reduce.5.cloned.1.call-done = f32[64,4,1024]{2,0,1:T(8,128)} async-done(((f32[64,4,1024]{2,0,1:T(8,128)}), f32[64,4,1024]{2,0,1:T(8,128)}) %all-reduce.5.cloned.1.call-update) | async-done | bytes 1048592 | tf_op jit(solution)/shard_map/psum | solution.py:22
  352.1 7.5 %fusion.10 = f32[4,64,16,80]{3,1,2,0:T(8,128)S(1)} fusion(bf16[16,4,80,1024]{3,2,1,0:T(8,128)(2,1)} %all-to-all-done, f32[64,4,1024]{2,0,1:T(8,128)} %all-reduce.5.cloned.1.call-done, f32[64,4]{0,1:T(4,128)S(1)} %broadcast_add_fusion.5), kind=kOutput, calls=%fused_computation.12 | convolution fusion | flops 671612928 | bytes 12846080 | tf_op jit(solution)/shard_map/oqmd,kqd->oqmk/dot_general | solution.py:53
  359.9 1.5 convert_reduce_fusion.2
  361.4 7.1 %convolution_bitcast_fusion.2 = f32[64,4,1024]{2,0,1:T(8,128)} fusion(bf16[16,4,80,1024]{3,2,1,0:T(8,128)(2,1)} %all-to-all-done, bf16[16,4,80,64]{2,3,0,1:T(8,128)(2,1)S(1)} %get-tuple-element.6), kind=kOutput, calls=%fused_computation.42 | convolution fusion | flops 671088640 | bytes 12189696 | tf_op jit(solution)/shard_map/oqmk,oqmd->kqd/dot_general | solution.py:60
  368.5 14.7 %psum.59 = f32[64,4]{0,1:T(4,128)S(1)} all-reduce(f32[64,4]{0,1:T(4,128)S(1)} %bitcast.115), channel_id=1, replica_groups=mesh['own'=16,'help'=8] {'help'}, use_global_device_ids=true, to_apply=%region_13.14 | all-reduce | flops 256 | bytes 2048 | tf_op jit(solution)/shard_map/psum | solution.py:22
  383.2 47.2 %all-reduce.7.cloned.1.call-done = f32[64,4,1024]{2,0,1:T(8,128)} async-done(((f32[64,4,1024]{2,0,1:T(8,128)}), f32[64,4,1024]{2,0,1:T(8,128)}) %all-reduce.7.cloned.1.call-update) | async-done | bytes 1048592 | tf_op jit(solution)/shard_map/psum | solution.py:22
  431.9 7.4 %fusion.8 = f32[4,64,16,80]{3,1,2,0:T(8,128)S(1)} fusion(bf16[16,4,80,1024]{3,2,1,0:T(8,128)(2,1)} %all-to-all-done, f32[64,4,1024]{2,0,1:T(8,128)} %all-reduce.7.cloned.1.call-done, f32[64,4]{0,1:T(4,128)S(1)} %broadcast_add_fusion.4), kind=kOutput, calls=%fused_computation.10 | convolution fusion | flops 671612928 | bytes 12846080 | tf_op jit(solution)/shard_map/oqmd,kqd->oqmk/dot_general | solution.py:53
  439.3 1.5 convert_reduce_fusion.1
  440.8 7.1 %convolution_bitcast_fusion.1 = f32[64,4,1024]{2,0,1:T(8,128)} fusion(bf16[16,4,80,1024]{3,2,1,0:T(8,128)(2,1)} %all-to-all-done, bf16[16,4,80,64]{2,3,0,1:T(8,128)(2,1)S(1)} %get-tuple-element.8), kind=kOutput, calls=%fused_computation.41 | convolution fusion | flops 671088640 | bytes 12189696 | tf_op jit(solution)/shard_map/oqmk,oqmd->kqd/dot_general | solution.py:60
  448.0 14.5 %psum.61 = f32[64,4]{0,1:T(4,128)S(1)} all-reduce(f32[64,4]{0,1:T(4,128)S(1)} %bitcast.116), channel_id=1, replica_groups=mesh['own'=16,'help'=8] {'help'}, use_global_device_ids=true, to_apply=%region_19.20 | all-reduce | flops 256 | bytes 2048 | tf_op jit(solution)/shard_map/psum | solution.py:22
  462.5 47.4 %all-reduce.9.cloned.1.call-done = f32[64,4,1024]{2,0,1:T(8,128)} async-done(((f32[64,4,1024]{2,0,1:T(8,128)}), f32[64,4,1024]{2,0,1:T(8,128)}) %all-reduce.9.cloned.1.call-update) | async-done | bytes 1048592 | tf_op jit(solution)/shard_map/psum | solution.py:22
  511.3 7.4 %fusion.6 = f32[4,64,16,80]{3,1,2,0:T(8,128)S(1)} fusion(bf16[16,4,80,1024]{3,2,1,0:T(8,128)(2,1)} %all-to-all-done, f32[64,4,1024]{2,0,1:T(8,128)} %all-reduce.9.cloned.1.call-done, f32[64,4]{0,1:T(4,128)S(1)} %broadcast_add_fusion.3), kind=kOutput, calls=%fused_computation.8 | convolution fusion | flops 671612928 | bytes 12846080 | tf_op jit(solution)/shard_map/oqmd,kqd->oqmk/dot_general | solution.py:53
  520.3 7.1 %convolution_bitcast_fusion = f32[64,4,1024]{2,0,1:T(8,128)} fusion(bf16[16,4,80,1024]{3,2,1,0:T(8,128)(2,1)} %all-to-all-done, bf16[16,4,80,64]{2,3,0,1:T(8,128)(2,1)S(1)} %get-tuple-element.10), kind=kOutput, calls=%fused_computation.40 | convolution fusion | flops 671088640 | bytes 12189696 | tf_op jit(solution)/shard_map/oqmk,oqmd->kqd/dot_general | solution.py:60
  527.4 14.5 %psum.63 = f32[64,4]{0,1:T(4,128)S(1)} all-reduce(f32[64,4]{0,1:T(4,128)S(1)} %bitcast.117), channel_id=1, replica_groups=mesh['own'=16,'help'=8] {'help'}, use_global_device_ids=true, to_apply=%region_25.26 | all-reduce | flops 256 | bytes 2048 | tf_op jit(solution)/shard_map/psum | solution.py:22
  541.9 47.5 %all-reduce.11.cloned.1.call-done = f32[64,4,1024]{2,0,1:T(8,128)} async-done(((f32[64,4,1024]{2,0,1:T(8,128)}), f32[64,4,1024]{2,0,1:T(8,128)}) %all-reduce.11.cloned.1.call-update) | async-done | bytes 1048592 | tf_op jit(solution)/shard_map/psum | solution.py:22
  590.7 1.7 copy.22
  (39 shorter events, 10.5 us)
Async XLA Ops:
  26.2 1.0 copy-start.1
  26.2 1.9 copy-start.2
  57.3 32.6 %all-to-all-start.1 = ((bf16[16,4,80]{2,1,0:T(4,128)(2,1)}), bf16[16,4,80]{2,1,0:T(4,128)(2,1)S(1)}, u32[]{:S(2)}, u32[]{:S(2)}) async-start(bf16[16,4,80]{2,1,0:T(4,128)(2,1)} %reshape.57), calls=%async_computation.1 | async-start | bytes 32768 | tf_op jit(solution)/shard_map/all_to_all | solution.py:45
  90.0 182.5 %all-to-all-start = ((bf16[16,4,80,1024]{3,2,1,0:T(8,128)(2,1)}), bf16[16,4,80,1024]{3,2,1,0:T(8,128)(2,1)}, u32[]{:S(2)}, u32[]{:S(2)}) async-start(bf16[16,4,80,1024]{3,2,1,0:T(8,128)(2,1)} %bitcast.102), calls=%async_computation | async-start | bytes 20971520 | tf_op jit(solution)/shard_map/all_to_all | solution.py:44
  96.6 255.5 %all-reduce.5.cloned.1.call-start = ((), (), s32[]{:S(2)}) async-start(), calls=%async_computation.2 | async-start | bytes 2097152 | tf_op jit(solution)/shard_map/psum | solution.py:22
  279.5 150.9 %all-reduce.7.cloned.1.call-start = ((), (), s32[]{:S(2)}) async-start(), calls=%async_computation.3 | async-start | bytes 2097152 | tf_op jit(solution)/shard_map/psum | solution.py:22
  352.1 7.5 %copy-start = (f32[64,4,1024]{2,0,1:T(8,128)S(1)}, f32[64,4,1024]{2,0,1:T(8,128)}, u32[]{:S(2)}) copy-start(f32[64,4,1024]{2,0,1:T(8,128)} %all-reduce.5.cloned.1.call-done) | copy-start | bytes 3145732
  368.5 141.4 %all-reduce.9.cloned.1.call-start = ((), (), s32[]{:S(2)}) async-start(), calls=%async_computation.4 | async-start | bytes 2097152 | tf_op jit(solution)/shard_map/psum | solution.py:22
  447.9 141.4 %all-reduce.11.cloned.1.call-start = ((), (), s32[]{:S(2)}) async-start(), calls=%async_computation.5 | async-start | bytes 2097152 | tf_op jit(solution)/shard_map/psum | solution.py:22
Sparse Core Ops, SparseCore 0:
  279.6 72.4 all-reduce.4
  368.6 61.7 all-reduce.6
  448.1 61.7 all-reduce.8
  527.5 61.7 all-reduce.10
where the time goes:
time: 602 us; the launch traced here: 599 us
  waiting for transfers between devices  374 us (62%)
  blocking collectives  59.6 us (10%)
  local copies, waits for them, and re-layouts  57 us (9%)
  matrix products  50.6 us (8%)
  other arithmetic  30.3 us (5%)
  starting transfers between devices  14.2 us (2%)
  between operations  13.3 us (2%)
    psum x4, waiting for transfers between devices, combine_help(): total, weight = lax.psum((sums, mass), 'help')  198 us
    all_to_all x1, waiting for transfers between devices, shards(): lax.all_to_all(outgoing, 'own', split_axis=0, concat_axis=0, tiled=True)  176 us
    psum x4, blocking collectives, combine_help(): total, weight = lax.psum((sums, mass), 'help')  59.6 us
    scatter x1, local copies, waits for them, and re-layouts, shards(): tagged = jnp.zeros((clusters * most,), jnp.bfloat16).at[slot].set((sub_in...  28.6 us
    scatter x1, local copies, waits for them, and re-layouts, shards(): jnp.zeros((clusters * most, width), jnp.bfloat16).at[slot].set(points)  25.3 us
    dot_general x3, matrix products, shards(): jnp.einsum('oqmd,kqd->oqmk', block, current16, preferred_element_type=jnp...  22.3 us
    dot_general x3, matrix products, shards(): jnp.einsum('oqmk,oqmd->kqd', weights, block, preferred_element_type=jnp.f...  21.3 us
    another operation x3, other arithmetic  19 us
  transfers between devices with their start and end apart: 6, of which 5 were waited for; matrix products, arithmetic and copies ran while one was open for 4% of the time, Pallas kernels for 0%

commit v1 on v0

v1 whole, which is shorter than its diff:
```python
import jax
import jax.numpy as jnp
from jax import lax
from jax.experimental import pallas as pl
from jax.experimental.pallas import tpu as pltpu
from jax.sharding import PartitionSpec as P

SUB = 64
ITERS = 3
CL_DEV = 4
CLUSTERS = 64
MOST = 80
GROUP = 4
WINDOW = 6

MESH = pl.DeviceIdType.MESH
NT = (((1,), (1,)), ((), ()))
f32, bf16, i32 = jnp.float32, jnp.bfloat16, jnp.int32


def link_loads(offset):
    loads = [0.0] * 6
    for axis, step in enumerate(offset):
        loads[2 * axis] += (step == 1) + (step == 2)
        loads[2 * axis + 1] += (step == 3) + (step == 2)
    return loads


def balanced_order():
    left = [(i // 16, i // 4 % 4, i % 4) for i in range(1, 64)]
    state = 12345
    shuffled = []
    while left:
        state = (state * 1103515245 + 12345) % 2**31
        shuffled.append(left.pop((state >> 8) % len(left)))
    left, loads, order = shuffled, [0.0] * 6, []
    while left:
        def unevenness(offset):
            after = [a + b for a, b in zip(loads, link_loads(offset))]
            return max(after) - sum(after) / 6
        best = min(left, key=unevenness)
        left.remove(best)
        order.append(best)
        loads = [a + b for a, b in zip(loads, link_loads(best))]
    return order + [(0, 0, 0)]


ORDER = balanced_order()


def kernel(x_hbm, label_ref, init_ref, out_ref,
           x, packed, block, pick, key, owner, tags, tags_in, live, weights,
           part, part_in, total, final,
           x_sem, own_sem, send, recv, tag_send, tag_recv, part_send, part_recv,
           fin_send, fin_recv, half_send, half_recv, out_sem):
    own, hlp = lax.axis_index("own"), lax.axis_index("help")
    cx, cz, cy, core = own // 4, own % 4, hlp // 2, hlp % 2
    sign = 1 + 2 * core

    def chip(dx, dy, dz):
        return (cx + dx * sign) % 4, (cy + dy * sign) % 4, (cz + dz * sign) % 4

    def device(px, py, pz):
        return (px * 4 + pz, py * 2 + core)

    sibling = (own, cy * 2 + 1 - core)

    barrier = pltpu.get_barrier_semaphore()

    @pl.loop(1, 64)
    def _(i):
        pl.semaphore_signal(barrier, inc=1, device_id=device(*chip(i // 16, i // 4 % 4, i % 4)),
                            device_id_type=MESH)
    pl.semaphore_signal(barrier, inc=1, device_id=sibling, device_id_type=MESH)

    load = pltpu.make_async_copy(x_hbm, x, x_sem)
    load.start()

    slot_id = lax.broadcasted_iota(i32, (CLUSTERS, 1), 0)
    owners = jnp.zeros((CLUSTERS, 1), i32)
    for i, offset in enumerate(ORDER):
        px, py, pz = chip(*offset)
        cluster = px * 16 + pz * 4 + py
        owner[i] = cluster
        owners = jnp.where(slot_id == i, cluster, owners)

    rows = lax.broadcasted_iota(i32, (256, 256), 0)
    cols = lax.broadcasted_iota(i32, (256, 256), 1)
    before = (rows < cols).astype(f32).astype(bf16)
    counts = jnp.zeros((CLUSTERS, 1), f32)
    tag = jnp.zeros((CLUSTERS, 128), f32)
    for j in range(16):
        label = label_ref[:, pl.ds(j * 256, 256)]
        member = (label == owners).astype(f32)
        earlier = jnp.dot(member.astype(bf16), before, preferred_element_type=f32) + counts
        counts = counts + jnp.sum(member, axis=1, keepdims=True)
        rank = jnp.sum(member * earlier, axis=0, keepdims=True).astype(i32)
        key[:, pl.ds(j * 256, 256)] = label * 128 + rank
        at_rank = (rank == lax.broadcasted_iota(i32, (128, 256), 0)).astype(f32).astype(bf16)
        mark = (member * (init_ref[:, pl.ds(j * 256, 256)] + 1).astype(f32)).astype(bf16)
        tag = tag + lax.dot_general(mark, at_rank, NT, preferred_element_type=f32)
    for i in range(CLUSTERS):
        tags[i] = jnp.broadcast_to(tag[i:i + 1, :], (8, 128))
    tags_in[CLUSTERS - 1] = jnp.broadcast_to(tag[CLUSTERS - 1:, :], (8, 128))

    load.wait()
    pl.semaphore_wait(barrier, 64)

    def rows_copy(i, target):
        return pltpu.make_async_remote_copy(
            src_ref=packed.at[i], dst_ref=block.at[i], send_sem=send.at[i], recv_sem=recv.at[i],
            device_id=target, device_id_type=MESH)

    def tags_copy(i, target):
        return pltpu.make_async_remote_copy(
            src_ref=tags.at[i], dst_ref=tags_in.at[i], send_sem=tag_send.at[i], recv_sem=tag_recv.at[i],
            device_id=target, device_id_type=MESH)

    @pl.loop(0, CLUSTERS // GROUP)
    def _(g):
        where = key[...]
        for j in range(GROUP):
            shifted = where - owner[g * GROUP + j] * 128
            pick[pl.ds(j * MOST, MOST), :] = (
                shifted == lax.broadcasted_iota(i32, (MOST, 1), 0)).astype(f32).astype(bf16)
        for n in range(4):
            moved = jnp.dot(pick[...], x[:, n * 256:(n + 1) * 256], preferred_element_type=f32)
            packed[pl.ds(g * GROUP, GROUP), :, n * 256:(n + 1) * 256] = (
                moved.astype(bf16).reshape(GROUP, MOST, 256))
        for j in range(GROUP):
            i = g * GROUP + j
            code = jnp.int32(0)
            for k in range(CLUSTERS // GROUP):
                ox, oy, oz = ORDER[k * GROUP + j]
                code = jnp.where(g == k, ox * 16 + oy * 4 + oz, code)
            target = device(*chip(code // 16, code // 4 % 4, code % 4))

            @pl.when(i >= WINDOW)
            def _():
                rows_copy(i - WINDOW, sibling).wait_send()
                tags_copy(i - WINDOW, sibling).wait_send()

            @pl.when(i < CLUSTERS - 1)
            def _():
                tags_copy(i, target).start()
                rows_copy(i, target).start()

    keep = pltpu.make_async_copy(packed.at[CLUSTERS - 1], block.at[CLUSTERS - 1], own_sem)
    keep.start()
    keep.wait()

    lane = lax.broadcasted_iota(i32, (128, 8 * MOST), 1)
    row = lax.broadcasted_iota(i32, (128, 8 * MOST), 0)
    spread = jnp.zeros((128, 8 * MOST), f32)
    for j in range(8):
        spread = jnp.where(lane - row == j * MOST, 1.0, spread)
    spread = jnp.where(row < MOST, spread, 0.0).astype(bf16)
    lane8 = lax.broadcasted_iota(i32, (8, 8 * MOST), 1) - MOST * lax.broadcasted_iota(i32, (8, 8 * MOST), 0)
    in_block = ((lane8 >= 0) & (lane8 < MOST)).astype(f32)
    total[...] = jnp.zeros_like(total)

    @pl.loop(0, 8)
    def _(g):
        for j in range(8):
            i = g * 8 + j

            @pl.when(i < CLUSTERS - 1)
            def _():
                tags_copy(i, sibling).wait_recv()
                rows_copy(i, sibling).wait_recv()
        marks = tags_in[pl.ds(g * 8, 8), 0, :].astype(bf16)
        mark = jnp.sum(jnp.dot(marks, spread, preferred_element_type=f32) * in_block,
                       axis=0, keepdims=True)
        start = pl.multiple_of(g * 8 * MOST, 128)
        live[0:1, pl.ds(start, 8 * MOST)] = (mark > 0.0).astype(f32)
        chosen = (mark.astype(i32) == lax.broadcasted_iota(i32, (SUB, 1), 0) + 1).astype(f32)
        data = block[pl.ds(g * 8, 8)].reshape(8 * MOST, 1024)
        total[:, :1024] += jnp.dot(chosen.astype(bf16), data, preferred_element_type=f32)
        total[:, 1024:] += sum(chosen[:, k * 128:(k + 1) * 128] for k in range(5))

    part[0, :, :1024] = total[:, :1024]
    part[0, :, 1024:] = jnp.broadcast_to(jnp.sum(total[:, 1024:], axis=1, keepdims=True), (SUB, 128))

    for k in range(WINDOW - 1):
        rows_copy(CLUSTERS - 1 - WINDOW + 1 + k, sibling).wait_send()
        tags_copy(CLUSTERS - 1 - WINDOW + 1 + k, sibling).wait_send()

    def combine(t):
        swap = pltpu.make_async_remote_copy(
            src_ref=part.at[t], dst_ref=part_in.at[t], send_sem=part_send.at[t], recv_sem=part_recv.at[t],
            device_id=sibling, device_id_type=MESH)
        swap.start()
        swap.wait()
        mass = part[t, :, 1024:1025] + part_in[t, :, 1024:1025]
        return (part[t, :, :1024] + part_in[t, :, :1024]) / (mass + 1.0)

    @pl.loop(0, ITERS)
    def _(t):
        current = combine(t)
        current16 = current.astype(bf16)
        squared = jnp.sum(current * current, axis=1, keepdims=True) * 0.125
        mass = jnp.zeros((SUB, 128), f32)
        for g in range(8):
            data = block[g * 8:(g + 1) * 8].reshape(8 * MOST, 1024)
            product = lax.dot_general(current16, data, NT, preferred_element_type=f32)
            score = product * 0.25 - squared
            grown = jnp.exp(score - jnp.max(score, axis=0, keepdims=True))
            alive = live[0:1, g * 8 * MOST:(g + 1) * 8 * MOST]
            weight = (grown / jnp.sum(grown, axis=0, keepdims=True) * alive).astype(bf16)
            weights[:, g * 8 * MOST:(g + 1) * 8 * MOST] = weight
            wide = weight.astype(f32)
            mass = mass + sum(wide[:, k * 128:(k + 1) * 128] for k in range(5))
        part[t + 1, :, 1024:] = jnp.broadcast_to(jnp.sum(mass, axis=1, keepdims=True), (SUB, 128))
        for n in range(4):
            data = block[:, :, n * 256:(n + 1) * 256].reshape(CLUSTERS * MOST, 256)
            part[t + 1, :, n * 256:(n + 1) * 256] = jnp.dot(
                weights[...], data, preferred_element_type=f32)

    final[cy] = combine(ITERS)

    half = pl.ds(core * 32, 32)

    def along(d):
        return pltpu.make_async_remote_copy(
            src_ref=final.at[cy, half], dst_ref=final.at[cy, half],
            send_sem=fin_send.at[d], recv_sem=fin_recv.at[d],
            device_id=(own, (cy + d) % 4 * 2 + core), device_id_type=MESH)

    def across(d):
        there = final.at[(cy + 4 - d) % 4, half]
        return pltpu.make_async_remote_copy(
            src_ref=there, dst_ref=there, send_sem=half_send.at[d], recv_sem=half_recv.at[d],
            device_id=sibling, device_id_type=MESH)

    for d in (1, 3, 2):
        along(d).start()
    for d in (1, 3, 2):
        along(d).wait_recv()
        across(d).start()
    for d in (1, 3, 2):
        along(d).wait_send()
        across(d).wait()
    store = pltpu.make_async_copy(final, out_ref, out_sem)
    store.start()
    store.wait()


def shards(points, cluster_of, sub_init):
    rows, width = points.shape
    dma = pltpu.SemaphoreType.DMA
    result = pl.pallas_call(
        kernel,
        out_shape=jax.ShapeDtypeStruct((CL_DEV, SUB, width), f32),
        in_specs=[pl.BlockSpec(memory_space=pl.ANY)] + [pl.BlockSpec(memory_space=pltpu.VMEM)] * 2,
        out_specs=pl.BlockSpec(memory_space=pl.ANY),
        scratch_shapes=[
            pltpu.VMEM((rows, width), bf16),
            pltpu.VMEM((CLUSTERS, MOST, width), bf16),
            pltpu.VMEM((CLUSTERS, MOST, width), bf16),
            pltpu.VMEM((GROUP * MOST, rows), bf16),
            pltpu.VMEM((1, rows), i32),
            pltpu.SMEM((CLUSTERS,), i32),
            pltpu.VMEM((CLUSTERS, 8, 128), f32),
            pltpu.VMEM((CLUSTERS, 8, 128), f32),
            pltpu.VMEM((8, CLUSTERS * MOST), f32),
            pltpu.VMEM((SUB, CLUSTERS * MOST), bf16),
            pltpu.VMEM((ITERS + 1, SUB, width + 128), f32),
            pltpu.VMEM((ITERS + 1, SUB, width + 128), f32),
            pltpu.VMEM((SUB, width + 128), f32),
            pltpu.VMEM((CL_DEV, SUB, width), f32),
            dma, dma, dma((CLUSTERS,)), dma((CLUSTERS,)), dma((CLUSTERS,)), dma((CLUSTERS,)),
            dma((ITERS + 1,)), dma((ITERS + 1,)),
            dma((4,)), dma((4,)), dma((4,)), dma((4,)), dma,
        ],
        compiler_params=pltpu.CompilerParams(
            collective_id=0, has_side_effects=True, vmem_limit_bytes=56 * 2**20),
    )(points, cluster_of.reshape(1, rows), sub_init.reshape(1, rows))
    return jnp.transpose(result, (1, 0, 2))


def solution(mesh):
    in_specs = (P(("own", "help"), None), P(("own", "help"), None), P(("own", "help")))
    out_specs = P(None, "own", None)
    return jax.shard_map(shards, mesh=mesh, in_specs=in_specs, out_specs=out_specs, check_vma=False)
```

time: 602 us -> 220 us (0.37)
  waiting for transfers between devices: 374 us -> 0 us
  Pallas kernels: 0 us -> 216 us
  blocking collectives: 59.6 us -> 0 us
  local copies, waits for them, and re-layouts: 57 us -> 2.87 us
  matrix products: 50.6 us -> 0 us
  other arithmetic: 30.3 us -> 0 us
  starting transfers between devices: 14.2 us -> 0 us
  between operations: 13.3 us -> 0.01 us
    pallas_call x0 -> x1, Pallas kernels: none -> 216 us  [shards(): pl.pallas_call(kernel, out_shape=jax.ShapeDtypeStruct((CL_DEV, SUB, width...]
    psum x4 -> x0, waiting for transfers between devices: 198 us -> none  [combine_help(): total, weight = lax.psum((sums, mass), 'help')]
    all_to_all x2 -> x0, waiting for transfers between devices: 176 us -> none  [the longest x1 176 us: shards(): lax.all_to_all(outgoing, 'own', split_axis=0, concat_axis=0, tiled=True)]
    psum x4 -> x0, blocking collectives: 59.6 us -> none  [combine_help(): total, weight = lax.psum((sums, mass), 'help')]
    scatter x2 -> x0, local copies, waits for them, and re-layouts: 53.8 us -> none  [the longest x1 28.6 us: shards(): tagged = jnp.zeros((clusters * most,), jnp.bfloat16).at[slot].set((sub_in...]
    dot_general x7 -> x0, matrix products: 50.6 us -> none  [the longest x3 22.3 us: shards(): jnp.einsum('oqmd,kqd->oqmk', block, current16, preferred_element_type=jnp...]
    another operation x3 -> x0, other arithmetic: 19 us -> none
    all_to_all x2 -> x0, starting transfers between devices: 14 us -> none  [the longest x1 7.33 us: shards(): lax.all_to_all(tagged, 'own', split_axis=0, concat_axis=0, tiled=True)]
  transfers between devices with their start and end apart: 6 -> 0, of which waited for: 5 -> 0; matrix products, arithmetic and copies ran while one was open for 4% -> 0% of each run, Pallas kernels for 0% -> 0%
where the time goes in v1:
time: 220 us; the launch traced here: 219 us
  Pallas kernels  216 us (98%)
  local copies, waits for them, and re-layouts  2.87 us (1%)
    pallas_call x1, Pallas kernels, shards(): pl.pallas_call(kernel, out_shape=jax.ShapeDtypeStruct((CL_DEV, SUB, width...  216 us

profile of v1, /device:TPU:33, one launch (start us, length us, event | category | flops | bytes accessed | tf_op | source)
XLA Modules:
  0.0 219.3 jit_solution(17174941168962069860)
XLA Ops:
  0.0 216.4 %shard_map.37 = f32[4,64,1024]{2,1,0:T(8,128)} custom-call(bf16[4096,1024]{1,0:T(8,128)(2,1)} %x_hbm.1, s32[1,4096]{1,0:T(1,128)} %bitcast.4, s32[1,4096]{1,0:T(1,128)} %bitcast.5), custom_call_target="tpu_custom_call" | custom-call | tf_op jit(solution)/shard_map/pallas_call | solution.py:251
  216.5 2.9 %copy.4 = f32[64,4,1024]{2,1,0:T(4,128)} copy(f32[64,4,1024]{2,0,1:T(8,128)} %bitcast.3) | data formatting | bytes 2097152 | tf_op jit(solution)/shard_map/transpose | solution.py:278

commit v2 on v1

--- a/solution.py
+++ b/solution.py
@@ -18,34 +18,12 @@
 f32, bf16, i32 = jnp.float32, jnp.bfloat16, jnp.int32
 
 
-def link_loads(offset):
-    loads = [0.0] * 6
-    for axis, step in enumerate(offset):
-        loads[2 * axis] += (step == 1) + (step == 2)
-        loads[2 * axis + 1] += (step == 3) + (step == 2)
-    return loads
-
-
-def balanced_order():
-    left = [(i // 16, i // 4 % 4, i % 4) for i in range(1, 64)]
-    state = 12345
-    shuffled = []
-    while left:
-        state = (state * 1103515245 + 12345) % 2**31
-        shuffled.append(left.pop((state >> 8) % len(left)))
-    left, loads, order = shuffled, [0.0] * 6, []
-    while left:
-        def unevenness(offset):
-            after = [a + b for a, b in zip(loads, link_loads(offset))]
-            return max(after) - sum(after) / 6
-        best = min(left, key=unevenness)
-        left.remove(best)
-        order.append(best)
-        loads = [a + b for a, b in zip(loads, link_loads(best))]
-    return order + [(0, 0, 0)]
-
-
-ORDER = balanced_order()
+CODES = [
+    42, 58, 16, 41, 3, 43, 1, 46, 4, 38, 12, 26, 48, 54, 28, 34, 8, 59, 17, 45, 7, 30, 52, 47, 5,
+    62, 20, 37, 15, 22, 60, 10, 32, 39, 13, 40, 2, 27, 49, 57, 19, 25, 51, 61, 23, 6, 44, 50, 24,
+    29, 55, 18, 56, 63, 21, 11, 33, 36, 14, 53, 31, 35, 9, 0,
+]
+ORDER = [(code // 16, code // 4 % 4, code % 4) for code in CODES]
 
 
 def kernel(x_hbm, label_ref, init_ref, out_ref,
@@ -104,11 +82,14 @@
     tags_in[CLUSTERS - 1] = jnp.broadcast_to(tag[CLUSTERS - 1:, :], (8, 128))
 
     load.wait()
-    pl.semaphore_wait(barrier, 64)
+
+    def slots(i):
+        return pl.ds(pl.multiple_of(i * MOST, 16), MOST)
 
     def rows_copy(i, target):
         return pltpu.make_async_remote_copy(
-            src_ref=packed.at[i], dst_ref=block.at[i], send_sem=send.at[i], recv_sem=recv.at[i],
+            src_ref=packed.at[slots(i)], dst_ref=block.at[slots(i)],
+            send_sem=send, recv_sem=recv.at[i],
             device_id=target, device_id_type=MESH)
 
     def tags_copy(i, target):
@@ -116,36 +97,47 @@
             src_ref=tags.at[i], dst_ref=tags_in.at[i], send_sem=tag_send.at[i], recv_sem=tag_recv.at[i],
             device_id=target, device_id_type=MESH)
 
-    @pl.loop(0, CLUSTERS // GROUP)
+    groups = CLUSTERS // GROUP
+
+    @pl.loop(0, groups + 1)
     def _(g):
-        where = key[...]
-        for j in range(GROUP):
-            shifted = where - owner[g * GROUP + j] * 128
-            pick[pl.ds(j * MOST, MOST), :] = (
-                shifted == lax.broadcasted_iota(i32, (MOST, 1), 0)).astype(f32).astype(bf16)
-        for n in range(4):
-            moved = jnp.dot(pick[...], x[:, n * 256:(n + 1) * 256], preferred_element_type=f32)
-            packed[pl.ds(g * GROUP, GROUP), :, n * 256:(n + 1) * 256] = (
-                moved.astype(bf16).reshape(GROUP, MOST, 256))
-        for j in range(GROUP):
-            i = g * GROUP + j
+        @pl.when(g < groups)
+        def _():
+            where = key[...]
+            for j in range(GROUP):
+                shifted = where - owner[g * GROUP + j] * 128
+                pick[pl.ds(j * MOST, MOST), :] = (
+                    shifted == lax.broadcasted_iota(i32, (MOST, 1), 0)).astype(f32).astype(bf16)
+
+        @pl.when(g == 1)
+        def _():
+            pl.semaphore_wait(barrier, 64)
+
+        for n in range(GROUP):
+            @pl.when(g < groups)
+            def _():
+                moved = jnp.dot(pick[...], x[:, n * 256:(n + 1) * 256], preferred_element_type=f32)
+                start = pl.multiple_of(g * GROUP * MOST, 16)
+                packed[pl.ds(start, GROUP * MOST), n * 256:(n + 1) * 256] = moved.astype(bf16)
+
+            i = (g - 1) * GROUP + n
             code = jnp.int32(0)
-            for k in range(CLUSTERS // GROUP):
-                ox, oy, oz = ORDER[k * GROUP + j]
-                code = jnp.where(g == k, ox * 16 + oy * 4 + oz, code)
+            for k in range(groups):
+                ox, oy, oz = ORDER[k * GROUP + n]
+                code = jnp.where(g == k + 1, ox * 16 + oy * 4 + oz, code)
             target = device(*chip(code // 16, code // 4 % 4, code % 4))
 
             @pl.when(i >= WINDOW)
             def _():
-                rows_copy(i - WINDOW, sibling).wait_send()
-                tags_copy(i - WINDOW, sibling).wait_send()
-
-            @pl.when(i < CLUSTERS - 1)
+                rows_copy(0, sibling).wait_send()
+
+            @pl.when((i >= 0) & (i < CLUSTERS - 1))
             def _():
                 tags_copy(i, target).start()
                 rows_copy(i, target).start()
 
-    keep = pltpu.make_async_copy(packed.at[CLUSTERS - 1], block.at[CLUSTERS - 1], own_sem)
+    keep = pltpu.make_async_copy(
+        packed.at[slots(CLUSTERS - 1)], block.at[slots(CLUSTERS - 1)], own_sem)
     keep.start()
     keep.wait()
 
@@ -174,16 +166,20 @@
         start = pl.multiple_of(g * 8 * MOST, 128)
         live[0:1, pl.ds(start, 8 * MOST)] = (mark > 0.0).astype(f32)
         chosen = (mark.astype(i32) == lax.broadcasted_iota(i32, (SUB, 1), 0) + 1).astype(f32)
-        data = block[pl.ds(g * 8, 8)].reshape(8 * MOST, 1024)
+        data = block[pl.ds(start, 8 * MOST), :]
         total[:, :1024] += jnp.dot(chosen.astype(bf16), data, preferred_element_type=f32)
         total[:, 1024:] += sum(chosen[:, k * 128:(k + 1) * 128] for k in range(5))
 
     part[0, :, :1024] = total[:, :1024]
     part[0, :, 1024:] = jnp.broadcast_to(jnp.sum(total[:, 1024:], axis=1, keepdims=True), (SUB, 128))
 
-    for k in range(WINDOW - 1):
-        rows_copy(CLUSTERS - 1 - WINDOW + 1 + k, sibling).wait_send()
-        tags_copy(CLUSTERS - 1 - WINDOW + 1 + k, sibling).wait_send()
+    @pl.loop(0, WINDOW - 1)
+    def _(k):
+        rows_copy(0, sibling).wait_send()
+
+    @pl.loop(0, CLUSTERS - 1)
+    def _(i):
+        tags_copy(i, sibling).wait_send()
 
     def combine(t):
         swap = pltpu.make_async_remote_copy(
@@ -201,7 +197,7 @@
         squared = jnp.sum(current * current, axis=1, keepdims=True) * 0.125
         mass = jnp.zeros((SUB, 128), f32)
         for g in range(8):
-            data = block[g * 8:(g + 1) * 8].reshape(8 * MOST, 1024)
+            data = block[g * 8 * MOST:(g + 1) * 8 * MOST, :]
             product = lax.dot_general(current16, data, NT, preferred_element_type=f32)
             score = product * 0.25 - squared
             grown = jnp.exp(score - jnp.max(score, axis=0, keepdims=True))
@@ -212,7 +208,7 @@
             mass = mass + sum(wide[:, k * 128:(k + 1) * 128] for k in range(5))
         part[t + 1, :, 1024:] = jnp.broadcast_to(jnp.sum(mass, axis=1, keepdims=True), (SUB, 128))
         for n in range(4):
-            data = block[:, :, n * 256:(n + 1) * 256].reshape(CLUSTERS * MOST, 256)
+            data = block[:, n * 256:(n + 1) * 256]
             part[t + 1, :, n * 256:(n + 1) * 256] = jnp.dot(
                 weights[...], data, preferred_element_type=f32)
 
@@ -255,8 +251,8 @@
         out_specs=pl.BlockSpec(memory_space=pl.ANY),
         scratch_shapes=[
             pltpu.VMEM((rows, width), bf16),
-            pltpu.VMEM((CLUSTERS, MOST, width), bf16),
-            pltpu.VMEM((CLUSTERS, MOST, width), bf16),
+            pltpu.VMEM((CLUSTERS * MOST, width), bf16),
+            pltpu.VMEM((CLUSTERS * MOST, width), bf16),
             pltpu.VMEM((GROUP * MOST, rows), bf16),
             pltpu.VMEM((1, rows), i32),
             pltpu.SMEM((CLUSTERS,), i32),
@@ -268,7 +264,7 @@
             pltpu.VMEM((ITERS + 1, SUB, width + 128), f32),
             pltpu.VMEM((SUB, width + 128), f32),
             pltpu.VMEM((CL_DEV, SUB, width), f32),
-            dma, dma, dma((CLUSTERS,)), dma((CLUSTERS,)), dma((CLUSTERS,)), dma((CLUSTERS,)),
+            dma, dma, dma, dma((CLUSTERS,)), dma((CLUSTERS,)), dma((CLUSTERS,)),
             dma((ITERS + 1,)), dma((ITERS + 1,)),
             dma((4,)), dma((4,)), dma((4,)), dma((4,)), dma,
         ],

time: 220 us -> 180 us (0.82)
  Pallas kernels: 216 us -> 175 us
    pallas_call x1, Pallas kernels: 216 us -> 175 us  [shards(): pl.pallas_call(kernel, out_shape=jax.ShapeDtypeStruct((CL_DEV, SUB, width...]
where the time goes in v2:
time: 180 us; the launch traced here: 177 us
  Pallas kernels  175 us (97%)
  local copies, waits for them, and re-layouts  2.87 us (2%)
    pallas_call x1, Pallas kernels, shards(): pl.pallas_call(kernel, out_shape=jax.ShapeDtypeStruct((CL_DEV, SUB, width...  175 us

profile of v2, /device:TPU:33, one launch (start us, length us, event | category | flops | bytes accessed | tf_op | source)
XLA Modules:
  0.0 177.4 jit_solution(11670816595438099413)
XLA Ops:
  0.0 174.5 %shard_map.37 = f32[4,64,1024]{2,1,0:T(8,128)} custom-call(bf16[4096,1024]{1,0:T(8,128)(2,1)} %x_hbm.1, s32[1,4096]{1,0:T(1,128)} %bitcast.4, s32[1,4096]{1,0:T(1,128)} %bitcast.5), custom_call_target="tpu_custom_call" | custom-call | tf_op jit(solution)/shard_map/pallas_call | solution.py:247
  174.5 2.9 %copy.4 = f32[64,4,1024]{2,1,0:T(4,128)} copy(f32[64,4,1024]{2,0,1:T(8,128)} %bitcast.3) | data formatting | bytes 2097152 | tf_op jit(solution)/shard_map/transpose | solution.py:274

commit v3 on v2

--- a/solution.py
+++ b/solution.py
@@ -12,6 +12,7 @@
 MOST = 80
 GROUP = 4
 WINDOW = 6
+QUARTERS = 4
 
 MESH = pl.DeviceIdType.MESH
 NT = (((1,), (1,)), ((), ()))
@@ -27,8 +28,8 @@
 
 
 def kernel(x_hbm, label_ref, init_ref, out_ref,
-           x, packed, block, pick, key, owner, tags, tags_in, live, weights,
-           part, part_in, total, final,
+           x, packed, block, turned, pick, key, owner, tags, tags_in, live, weights,
+           part, part_in, mass, mass_in, centre, final,
            x_sem, own_sem, send, recv, tag_send, tag_recv, part_send, part_recv,
            fin_send, fin_recv, half_send, half_recv, out_sem):
     own, hlp = lax.axis_index("own"), lax.axis_index("help")
@@ -149,7 +150,8 @@
     spread = jnp.where(row < MOST, spread, 0.0).astype(bf16)
     lane8 = lax.broadcasted_iota(i32, (8, 8 * MOST), 1) - MOST * lax.broadcasted_iota(i32, (8, 8 * MOST), 0)
     in_block = ((lane8 >= 0) & (lane8 < MOST)).astype(f32)
-    total[...] = jnp.zeros_like(total)
+    part[0] = jnp.zeros_like(part[0])
+    mass[0] = jnp.zeros_like(mass[0])
 
     @pl.loop(0, 8)
     def _(g):
@@ -167,11 +169,110 @@
         live[0:1, pl.ds(start, 8 * MOST)] = (mark > 0.0).astype(f32)
         chosen = (mark.astype(i32) == lax.broadcasted_iota(i32, (SUB, 1), 0) + 1).astype(f32)
         data = block[pl.ds(start, 8 * MOST), :]
-        total[:, :1024] += jnp.dot(chosen.astype(bf16), data, preferred_element_type=f32)
-        total[:, 1024:] += sum(chosen[:, k * 128:(k + 1) * 128] for k in range(5))
-
-    part[0, :, :1024] = total[:, :1024]
-    part[0, :, 1024:] = jnp.broadcast_to(jnp.sum(total[:, 1024:], axis=1, keepdims=True), (SUB, 128))
+        turned[:, pl.ds(start, 8 * MOST)] = data.T
+        for n in range(QUARTERS):
+            part[0, n] += jnp.dot(chosen.astype(bf16), data[:, n * 256:(n + 1) * 256],
+                                  preferred_element_type=f32)
+        mass[0] += sum(chosen[:, k * 128:(k + 1) * 128] for k in range(5))
+
+    def swap(t, n):
+        return pltpu.make_async_remote_copy(
+            src_ref=part.at[t, n], dst_ref=part_in.at[t, n],
+            send_sem=part_send.at[t * 5 + n], recv_sem=part_recv.at[t * 5 + n],
+            device_id=sibling, device_id_type=MESH)
+
+    def swap_mass(t):
+        return pltpu.make_async_remote_copy(
+            src_ref=mass.at[t], dst_ref=mass_in.at[t],
+            send_sem=part_send.at[t * 5 + 4], recv_sem=part_recv.at[t * 5 + 4],
+            device_id=sibling, device_id_type=MESH)
+
+    def divisor(t):
+        swap_mass(t).wait_recv()
+        return jnp.sum(mass[t] + mass_in[t], axis=1, keepdims=True) + 1.0
+
+    def combine(t, n, below):
+        swap(t, n).wait_recv()
+        current = (part[t, n] + part_in[t, n]) / below
+        final[cy, n] = current
+        centre[:, n * 256:(n + 1) * 256] = current.astype(bf16)
+        return jnp.sum(current * current, axis=1, keepdims=True)
+
+    half = pl.ds(core * 32, 32)
+
+    def along(d, n):
+        return pltpu.make_async_remote_copy(
+            src_ref=final.at[cy, n, half], dst_ref=final.at[cy, n, half],
+            send_sem=fin_send.at[d * 4 + n], recv_sem=fin_recv.at[d * 4 + n],
+            device_id=(own, (cy + d) % 4 * 2 + core), device_id_type=MESH)
+
+    def across(d, n):
+        there = final.at[(cy + 4 - d) % 4, n, half]
+        return pltpu.make_async_remote_copy(
+            src_ref=there, dst_ref=there,
+            send_sem=half_send.at[d * 4 + n], recv_sem=half_recv.at[d * 4 + n],
+            device_id=sibling, device_id_type=MESH)
+
+    def store(d, n):
+        j = (cy + 4 - d) % 4
+        return pltpu.make_async_copy(
+            final.at[j, n], out_ref.at[j, :, pl.ds(n * 256, 256)], out_sem.at[d * 4 + n])
+
+    swap_mass(0).start()
+    for n in range(QUARTERS):
+        swap(0, n).start()
+    below = divisor(0)
+    squared = jnp.zeros((SUB, 1), f32)
+    for n in range(QUARTERS):
+        squared = squared + combine(0, n, below)
+
+    def iteration(t, squared):
+        bias = squared * 0.125
+        heavy = jnp.zeros((SUB, 128), f32)
+        for g in range(8):
+            lanes = slice(g * 8 * MOST, (g + 1) * 8 * MOST)
+            product = jnp.dot(centre[...], turned[:, lanes], preferred_element_type=f32)
+            score = product * 0.25 - bias
+            grown = jnp.exp(score - jnp.max(score, axis=0, keepdims=True))
+            weight = (grown / jnp.sum(grown, axis=0, keepdims=True) * live[0:1, lanes]).astype(bf16)
+            weights[:, lanes] = weight
+            wide = weight.astype(f32)
+            heavy = heavy + sum(wide[:, k * 128:(k + 1) * 128] for k in range(5))
+        mass[t + 1] = heavy
+        swap_mass(t + 1).start()
+
+        def finish(n, below):
+            after = combine(t + 1, n, below)
+
+            @pl.when(t == ITERS - 1)
+            def _():
+                for d in (1, 3, 2):
+                    along(d, n).start()
+            return after
+
+        squared = jnp.zeros((SUB, 1), f32)
+        for n in range(QUARTERS):
+            part[t + 1, n] = jnp.dot(weights[...], block[:, n * 256:(n + 1) * 256],
+                                     preferred_element_type=f32)
+            swap(t + 1, n).start()
+            if n == 0:
+                below = divisor(t + 1)
+            else:
+                squared = squared + finish(n - 1, below)
+        return squared + finish(QUARTERS - 1, below)
+
+    lax.fori_loop(0, ITERS, iteration, squared)
+
+    for n in range(QUARTERS):
+        store(0, n).start()
+    for n in range(QUARTERS):
+        for d in (1, 3, 2):
+            along(d, n).wait_recv()
+            across(d, n).start()
+    for n in range(QUARTERS):
+        for d in (1, 3, 2):
+            across(d, n).wait_recv()
+            store(d, n).start()
 
     @pl.loop(0, WINDOW - 1)
     def _(k):
@@ -181,64 +282,16 @@
     def _(i):
         tags_copy(i, sibling).wait_send()
 
-    def combine(t):
-        swap = pltpu.make_async_remote_copy(
-            src_ref=part.at[t], dst_ref=part_in.at[t], send_sem=part_send.at[t], recv_sem=part_recv.at[t],
-            device_id=sibling, device_id_type=MESH)
-        swap.start()
-        swap.wait()
-        mass = part[t, :, 1024:1025] + part_in[t, :, 1024:1025]
-        return (part[t, :, :1024] + part_in[t, :, :1024]) / (mass + 1.0)
-
-    @pl.loop(0, ITERS)
-    def _(t):
-        current = combine(t)
-        current16 = current.astype(bf16)
-        squared = jnp.sum(current * current, axis=1, keepdims=True) * 0.125
-        mass = jnp.zeros((SUB, 128), f32)
-        for g in range(8):
-            data = block[g * 8 * MOST:(g + 1) * 8 * MOST, :]
-            product = lax.dot_general(current16, data, NT, preferred_element_type=f32)
-            score = product * 0.25 - squared
-            grown = jnp.exp(score - jnp.max(score, axis=0, keepdims=True))
-            alive = live[0:1, g * 8 * MOST:(g + 1) * 8 * MOST]
-            weight = (grown / jnp.sum(grown, axis=0, keepdims=True) * alive).astype(bf16)
-            weights[:, g * 8 * MOST:(g + 1) * 8 * MOST] = weight
-            wide = weight.astype(f32)
-            mass = mass + sum(wide[:, k * 128:(k + 1) * 128] for k in range(5))
-        part[t + 1, :, 1024:] = jnp.broadcast_to(jnp.sum(mass, axis=1, keepdims=True), (SUB, 128))
-        for n in range(4):
-            data = block[:, n * 256:(n + 1) * 256]
-            part[t + 1, :, n * 256:(n + 1) * 256] = jnp.dot(
-                weights[...], data, preferred_element_type=f32)
-
-    final[cy] = combine(ITERS)
-
-    half = pl.ds(core * 32, 32)
-
-    def along(d):
-        return pltpu.make_async_remote_copy(
-            src_ref=final.at[cy, half], dst_ref=final.at[cy, half],
-            send_sem=fin_send.at[d], recv_sem=fin_recv.at[d],
-            device_id=(own, (cy + d) % 4 * 2 + core), device_id_type=MESH)
-
-    def across(d):
-        there = final.at[(cy + 4 - d) % 4, half]
-        return pltpu.make_async_remote_copy(
-            src_ref=there, dst_ref=there, send_sem=half_send.at[d], recv_sem=half_recv.at[d],
-            device_id=sibling, device_id_type=MESH)
-
-    for d in (1, 3, 2):
-        along(d).start()
-    for d in (1, 3, 2):
-        along(d).wait_recv()
-        across(d).start()
-    for d in (1, 3, 2):
-        along(d).wait_send()
-        across(d).wait()
-    store = pltpu.make_async_copy(final, out_ref, out_sem)
-    store.start()
-    store.wait()
+    for t in range(ITERS + 1):
+        swap_mass(t).wait_send()
+        for n in range(QUARTERS):
+            swap(t, n).wait_send()
+    for n in range(QUARTERS):
+        store(0, n).wait()
+        for d in (1, 3, 2):
+            along(d, n).wait_send()
+            across(d, n).wait_send()
+            store(d, n).wait()
 
 
 def shards(points, cluster_of, sub_init):
@@ -253,6 +306,7 @@
             pltpu.VMEM((rows, width), bf16),
             pltpu.VMEM((CLUSTERS * MOST, width), bf16),
             pltpu.VMEM((CLUSTERS * MOST, width), bf16),
+            pltpu.VMEM((width, CLUSTERS * MOST), bf16),
             pltpu.VMEM((GROUP * MOST, rows), bf16),
             pltpu.VMEM((1, rows), i32),
             pltpu.SMEM((CLUSTERS,), i32),
@@ -260,13 +314,15 @@
             pltpu.VMEM((CLUSTERS, 8, 128), f32),
             pltpu.VMEM((8, CLUSTERS * MOST), f32),
             pltpu.VMEM((SUB, CLUSTERS * MOST), bf16),
-            pltpu.VMEM((ITERS + 1, SUB, width + 128), f32),
-            pltpu.VMEM((ITERS + 1, SUB, width + 128), f32),
-            pltpu.VMEM((SUB, width + 128), f32),
-            pltpu.VMEM((CL_DEV, SUB, width), f32),
+            pltpu.VMEM((ITERS + 1, QUARTERS, SUB, 256), f32),
+            pltpu.VMEM((ITERS + 1, QUARTERS, SUB, 256), f32),
+            pltpu.VMEM((ITERS + 1, SUB, 128), f32),
+            pltpu.VMEM((ITERS + 1, SUB, 128), f32),
+            pltpu.VMEM((SUB, width), bf16),
+            pltpu.VMEM((CL_DEV, QUARTERS, SUB, 256), f32),
             dma, dma, dma, dma((CLUSTERS,)), dma((CLUSTERS,)), dma((CLUSTERS,)),
-            dma((ITERS + 1,)), dma((ITERS + 1,)),
-            dma((4,)), dma((4,)), dma((4,)), dma((4,)), dma,
+            dma((5 * (ITERS + 1),)), dma((5 * (ITERS + 1),)),
+            dma((16,)), dma((16,)), dma((16,)), dma((16,)), dma((16,)),
         ],
         compiler_params=pltpu.CompilerParams(
             collective_id=0, has_side_effects=True, vmem_limit_bytes=56 * 2**20),

time: 180 us -> 179 us (level)
  Pallas kernels: 175 us -> 173 us
where the time goes in v3:
time: 179 us; the launch traced here: 176 us
  Pallas kernels  173 us (97%)
  local copies, waits for them, and re-layouts  2.87 us (2%)
    pallas_call x1, Pallas kernels, shards(): pl.pallas_call(kernel, out_shape=jax.ShapeDtypeStruct((CL_DEV, SUB, width...  173 us

profile of v3, /device:TPU:33, one launch (start us, length us, event | category | flops | bytes accessed | tf_op | source)
XLA Modules:
  0.0 176.4 jit_solution(2575418491527482010)
XLA Ops:
  0.0 173.5 %shard_map.37 = f32[4,64,1024]{2,1,0:T(8,128)} custom-call(bf16[4096,1024]{1,0:T(8,128)(2,1)} %x_hbm.1, s32[1,4096]{1,0:T(1,128)} %bitcast.4, s32[1,4096]{1,0:T(1,128)} %bitcast.5), custom_call_target="tpu_custom_call" | custom-call | tf_op jit(solution)/shard_map/pallas_call | solution.py:300
  173.5 2.9 %copy.4 = f32[64,4,1024]{2,1,0:T(4,128)} copy(f32[64,4,1024]{2,0,1:T(8,128)} %bitcast.3) | data formatting | bytes 2097152 | tf_op jit(solution)/shard_map/transpose | solution.py:330

commit v4 on v3

--- a/solution.py
+++ b/solution.py
@@ -11,8 +11,9 @@
 CLUSTERS = 64
 MOST = 80
 GROUP = 4
-WINDOW = 6
-QUARTERS = 4
+WINDOW = 7
+PARTS = 2
+WIDE = 512
 
 MESH = pl.DeviceIdType.MESH
 NT = (((1,), (1,)), ((), ()))
@@ -102,25 +103,11 @@
 
     @pl.loop(0, groups + 1)
     def _(g):
-        @pl.when(g < groups)
-        def _():
-            where = key[...]
-            for j in range(GROUP):
-                shifted = where - owner[g * GROUP + j] * 128
-                pick[pl.ds(j * MOST, MOST), :] = (
-                    shifted == lax.broadcasted_iota(i32, (MOST, 1), 0)).astype(f32).astype(bf16)
-
         @pl.when(g == 1)
         def _():
             pl.semaphore_wait(barrier, 64)
 
         for n in range(GROUP):
-            @pl.when(g < groups)
-            def _():
-                moved = jnp.dot(pick[...], x[:, n * 256:(n + 1) * 256], preferred_element_type=f32)
-                start = pl.multiple_of(g * GROUP * MOST, 16)
-                packed[pl.ds(start, GROUP * MOST), n * 256:(n + 1) * 256] = moved.astype(bf16)
-
             i = (g - 1) * GROUP + n
             code = jnp.int32(0)
             for k in range(groups):
@@ -136,6 +123,18 @@
             def _():
                 tags_copy(i, target).start()
                 rows_copy(i, target).start()
+
+            @pl.when(g < groups)
+            def _():
+                if n == 0:
+                    where = key[...]
+                    for j in range(GROUP):
+                        shifted = where - owner[g * GROUP + j] * 128
+                        pick[pl.ds(j * MOST, MOST), :] = (
+                            shifted == lax.broadcasted_iota(i32, (MOST, 1), 0)).astype(f32).astype(bf16)
+                moved = jnp.dot(pick[...], x[:, n * 256:(n + 1) * 256], preferred_element_type=f32)
+                start = pl.multiple_of(g * GROUP * MOST, 16)
+                packed[pl.ds(start, GROUP * MOST), n * 256:(n + 1) * 256] = moved.astype(bf16)
 
     keep = pltpu.make_async_copy(
         packed.at[slots(CLUSTERS - 1)], block.at[slots(CLUSTERS - 1)], own_sem)
@@ -170,21 +169,21 @@
         chosen = (mark.astype(i32) == lax.broadcasted_iota(i32, (SUB, 1), 0) + 1).astype(f32)
         data = block[pl.ds(start, 8 * MOST), :]
         turned[:, pl.ds(start, 8 * MOST)] = data.T
-        for n in range(QUARTERS):
-            part[0, n] += jnp.dot(chosen.astype(bf16), data[:, n * 256:(n + 1) * 256],
+        for n in range(PARTS):
+            part[0, n] += jnp.dot(chosen.astype(bf16), data[:, n * WIDE:(n + 1) * WIDE],
                                   preferred_element_type=f32)
         mass[0] += sum(chosen[:, k * 128:(k + 1) * 128] for k in range(5))
 
     def swap(t, n):
         return pltpu.make_async_remote_copy(
             src_ref=part.at[t, n], dst_ref=part_in.at[t, n],
-            send_sem=part_send.at[t * 5 + n], recv_sem=part_recv.at[t * 5 + n],
+            send_sem=part_send.at[t * 3 + n], recv_sem=part_recv.at[t * 3 + n],
             device_id=sibling, device_id_type=MESH)
 
     def swap_mass(t):
         return pltpu.make_async_remote_copy(
             src_ref=mass.at[t], dst_ref=mass_in.at[t],
-            send_sem=part_send.at[t * 5 + 4], recv_sem=part_recv.at[t * 5 + 4],
+            send_sem=part_send.at[t * 3 + 2], recv_sem=part_recv.at[t * 3 + 2],
             device_id=sibling, device_id_type=MESH)
 
     def divisor(t):
@@ -195,7 +194,7 @@
         swap(t, n).wait_recv()
         current = (part[t, n] + part_in[t, n]) / below
         final[cy, n] = current
-        centre[:, n * 256:(n + 1) * 256] = current.astype(bf16)
+        centre[:, n * WIDE:(n + 1) * WIDE] = current.astype(bf16)
         return jnp.sum(current * current, axis=1, keepdims=True)
 
     half = pl.ds(core * 32, 32)
@@ -203,27 +202,27 @@
     def along(d, n):
         return pltpu.make_async_remote_copy(
             src_ref=final.at[cy, n, half], dst_ref=final.at[cy, n, half],
-            send_sem=fin_send.at[d * 4 + n], recv_sem=fin_recv.at[d * 4 + n],
+            send_sem=fin_send.at[d * 2 + n], recv_sem=fin_recv.at[d * 2 + n],
             device_id=(own, (cy + d) % 4 * 2 + core), device_id_type=MESH)
 
     def across(d, n):
         there = final.at[(cy + 4 - d) % 4, n, half]
         return pltpu.make_async_remote_copy(
             src_ref=there, dst_ref=there,
-            send_sem=half_send.at[d * 4 + n], recv_sem=half_recv.at[d * 4 + n],
+            send_sem=half_send.at[d * 2 + n], recv_sem=half_recv.at[d * 2 + n],
             device_id=sibling, device_id_type=MESH)
 
     def store(d, n):
         j = (cy + 4 - d) % 4
         return pltpu.make_async_copy(
-            final.at[j, n], out_ref.at[j, :, pl.ds(n * 256, 256)], out_sem.at[d * 4 + n])
+            final.at[j, n], out_ref.at[j, :, pl.ds(n * WIDE, WIDE)], out_sem.at[d * 2 + n])
 
     swap_mass(0).start()
-    for n in range(QUARTERS):
+    for n in range(PARTS):
         swap(0, n).start()
     below = divisor(0)
     squared = jnp.zeros((SUB, 1), f32)
-    for n in range(QUARTERS):
+    for n in range(PARTS):
         squared = squared + combine(0, n, below)
 
     def iteration(t, squared):
@@ -251,25 +250,25 @@
             return after
 
         squared = jnp.zeros((SUB, 1), f32)
-        for n in range(QUARTERS):
-            part[t + 1, n] = jnp.dot(weights[...], block[:, n * 256:(n + 1) * 256],
+        for n in range(PARTS):
+            part[t + 1, n] = jnp.dot(weights[...], block[:, n * WIDE:(n + 1) * WIDE],
                                      preferred_element_type=f32)
             swap(t + 1, n).start()
             if n == 0:
                 below = divisor(t + 1)
             else:
                 squared = squared + finish(n - 1, below)
-        return squared + finish(QUARTERS - 1, below)
+        return squared + finish(PARTS - 1, below)
 
     lax.fori_loop(0, ITERS, iteration, squared)
 
-    for n in range(QUARTERS):
+    for n in range(PARTS):
         store(0, n).start()
-    for n in range(QUARTERS):
+    for n in range(PARTS):
         for d in (1, 3, 2):
             along(d, n).wait_recv()
             across(d, n).start()
-    for n in range(QUARTERS):
+    for n in range(PARTS):
         for d in (1, 3, 2):
             across(d, n).wait_recv()
             store(d, n).start()
@@ -284,9 +283,9 @@
 
     for t in range(ITERS + 1):
         swap_mass(t).wait_send()
-        for n in range(QUARTERS):
+        for n in range(PARTS):
             swap(t, n).wait_send()
-    for n in range(QUARTERS):
+    for n in range(PARTS):
         store(0, n).wait()
         for d in (1, 3, 2):
             along(d, n).wait_send()
@@ -314,15 +313,15 @@
             pltpu.VMEM((CLUSTERS, 8, 128), f32),
             pltpu.VMEM((8, CLUSTERS * MOST), f32),
             pltpu.VMEM((SUB, CLUSTERS * MOST), bf16),
-            pltpu.VMEM((ITERS + 1, QUARTERS, SUB, 256), f32),
-            pltpu.VMEM((ITERS + 1, QUARTERS, SUB, 256), f32),
+            pltpu.VMEM((ITERS + 1, PARTS, SUB, WIDE), f32),
+            pltpu.VMEM((ITERS + 1, PARTS, SUB, WIDE), f32),
             pltpu.VMEM((ITERS + 1, SUB, 128), f32),
             pltpu.VMEM((ITERS + 1, SUB, 128), f32),
             pltpu.VMEM((SUB, width), bf16),
-            pltpu.VMEM((CL_DEV, QUARTERS, SUB, 256), f32),
+            pltpu.VMEM((CL_DEV, PARTS, SUB, WIDE), f32),
             dma, dma, dma, dma((CLUSTERS,)), dma((CLUSTERS,)), dma((CLUSTERS,)),
-            dma((5 * (ITERS + 1),)), dma((5 * (ITERS + 1),)),
-            dma((16,)), dma((16,)), dma((16,)), dma((16,)), dma((16,)),
+            dma((3 * (ITERS + 1),)), dma((3 * (ITERS + 1),)),
+            dma((8,)), dma((8,)), dma((8,)), dma((8,)), dma((8,)),
         ],
         compiler_params=pltpu.CompilerParams(
             collective_id=0, has_side_effects=True, vmem_limit_bytes=56 * 2**20),

time: 179 us -> 174 us (0.972)
  Pallas kernels: 173 us -> 168 us
    pallas_call x1, Pallas kernels: 173 us -> 168 us  [shards(): pl.pallas_call(kernel, out_shape=jax.ShapeDtypeStruct((CL_DEV, SUB, width...]
where the time goes in v4:
time: 174 us; the launch traced here: 171 us
  Pallas kernels  168 us (97%)
  local copies, waits for them, and re-layouts  2.87 us (2%)
    pallas_call x1, Pallas kernels, shards(): pl.pallas_call(kernel, out_shape=jax.ShapeDtypeStruct((CL_DEV, SUB, width...  168 us

profile of v4, /device:TPU:33, one launch (start us, length us, event | category | flops | bytes accessed | tf_op | source)
XLA Modules:
  0.0 171.1 jit_solution(4701614860449457139)
XLA Ops:
  0.0 168.2 %shard_map.37 = f32[4,64,1024]{2,1,0:T(8,128)} custom-call(bf16[4096,1024]{1,0:T(8,128)(2,1)} %x_hbm.1, s32[1,4096]{1,0:T(1,128)} %bitcast.4, s32[1,4096]{1,0:T(1,128)} %bitcast.5), custom_call_target="tpu_custom_call" | custom-call | tf_op jit(solution)/shard_map/pallas_call | solution.py:299
  168.2 2.9 %copy.4 = f32[64,4,1024]{2,1,0:T(4,128)} copy(f32[64,4,1024]{2,0,1:T(8,128)} %bitcast.3) | data formatting | bytes 2097152 | tf_op jit(solution)/shard_map/transpose | solution.py:329

commit v5 on v4

--- a/solution.py
+++ b/solution.py
@@ -45,16 +45,14 @@
 
     sibling = (own, cy * 2 + 1 - core)
 
-    barrier = pltpu.get_barrier_semaphore()
-
-    @pl.loop(1, 64)
-    def _(i):
-        pl.semaphore_signal(barrier, inc=1, device_id=device(*chip(i // 16, i // 4 % 4, i % 4)),
-                            device_id_type=MESH)
-    pl.semaphore_signal(barrier, inc=1, device_id=sibling, device_id_type=MESH)
-
     load = pltpu.make_async_copy(x_hbm, x, x_sem)
     load.start()
+
+    barrier = pltpu.get_barrier_semaphore()
+    xs, ys, zs = ([(c + d) % 4 for d in range(4)] for c in (cx, cy, cz))
+    for dx, dy, dz in sorted(ORDER[:-1], key=lambda o: -sum(min(d, 4 - d) for d in o)):
+        pl.semaphore_signal(barrier, inc=1, device_id=device(xs[dx], ys[dy], zs[dz]), device_id_type=MESH)
+    pl.semaphore_signal(barrier, inc=1, device_id=sibling, device_id_type=MESH)
 
     slot_id = lax.broadcasted_iota(i32, (CLUSTERS, 1), 0)
     owners = jnp.zeros((CLUSTERS, 1), i32)
@@ -152,8 +150,16 @@
     part[0] = jnp.zeros_like(part[0])
     mass[0] = jnp.zeros_like(mass[0])
 
+    def turn(g):
+        rows = pl.ds(pl.multiple_of(g * 8 * MOST, 128), 8 * MOST)
+        turned[:, rows] = block[rows, :].T
+
     @pl.loop(0, 8)
     def _(g):
+        @pl.when(g > 0)
+        def _():
+            turn(g - 1)
+
         for j in range(8):
             i = g * 8 + j
 
@@ -168,7 +174,6 @@
         live[0:1, pl.ds(start, 8 * MOST)] = (mark > 0.0).astype(f32)
         chosen = (mark.astype(i32) == lax.broadcasted_iota(i32, (SUB, 1), 0) + 1).astype(f32)
         data = block[pl.ds(start, 8 * MOST), :]
-        turned[:, pl.ds(start, 8 * MOST)] = data.T
         for n in range(PARTS):
             part[0, n] += jnp.dot(chosen.astype(bf16), data[:, n * WIDE:(n + 1) * WIDE],
                                   preferred_element_type=f32)
@@ -220,6 +225,7 @@
     swap_mass(0).start()
     for n in range(PARTS):
         swap(0, n).start()
+    turn(7)
     below = divisor(0)
     squared = jnp.zeros((SUB, 1), f32)
     for n in range(PARTS):
@@ -245,7 +251,7 @@
 
             @pl.when(t == ITERS - 1)
             def _():
-                for d in (1, 3, 2):
+                for d in (2, 1, 3):
                     along(d, n).start()
             return after
 
@@ -264,14 +270,6 @@
 
     for n in range(PARTS):
         store(0, n).start()
-    for n in range(PARTS):
-        for d in (1, 3, 2):
-            along(d, n).wait_recv()
-            across(d, n).start()
-    for n in range(PARTS):
-        for d in (1, 3, 2):
-            across(d, n).wait_recv()
-            store(d, n).start()
 
     @pl.loop(0, WINDOW - 1)
     def _(k):
@@ -285,6 +283,15 @@
         swap_mass(t).wait_send()
         for n in range(PARTS):
             swap(t, n).wait_send()
+    for n in range(PARTS):
+        for d in (1, 3, 2):
+            along(d, n).wait_recv()
+            across(d, n).start()
+    for n in range(PARTS):
+        for d in (1, 3, 2):
+            across(d, n).wait_recv()
+            store(d, n).start()
+
     for n in range(PARTS):
         store(0, n).wait()
         for d in (1, 3, 2):

time: 174 us -> 172 us (0.989)
  Pallas kernels: 168 us -> 166 us
    pallas_call x1, Pallas kernels: 168 us -> 166 us  [shards(): pl.pallas_call(kernel, out_shape=jax.ShapeDtypeStruct((CL_DEV, SUB, width...]
where the time goes in v5:
time: 172 us; the launch traced here: 169 us
  Pallas kernels  166 us (97%)
  local copies, waits for them, and re-layouts  2.87 us (2%)
    pallas_call x1, Pallas kernels, shards(): pl.pallas_call(kernel, out_shape=jax.ShapeDtypeStruct((CL_DEV, SUB, width...  166 us

profile of v5, /device:TPU:33, one launch (start us, length us, event | category | flops | bytes accessed | tf_op | source)
XLA Modules:
  0.0 169.3 jit_solution(3742587651159934684)
XLA Ops:
  0.0 166.4 %shard_map.37 = f32[4,64,1024]{2,1,0:T(8,128)} custom-call(bf16[4096,1024]{1,0:T(8,128)(2,1)} %x_hbm.1, s32[1,4096]{1,0:T(1,128)} %bitcast.4, s32[1,4096]{1,0:T(1,128)} %bitcast.5), custom_call_target="tpu_custom_call" | custom-call | tf_op jit(solution)/shard_map/pallas_call | solution.py:306
  166.4 2.9 %copy.4 = f32[64,4,1024]{2,1,0:T(4,128)} copy(f32[64,4,1024]{2,0,1:T(8,128)} %bitcast.3) | data formatting | bytes 2097152 | tf_op jit(solution)/shard_map/transpose | solution.py:336

commit v6 on v5

--- a/solution.py
+++ b/solution.py
@@ -30,7 +30,7 @@
 
 def kernel(x_hbm, label_ref, init_ref, out_ref,
            x, packed, block, turned, pick, key, owner, tags, tags_in, live, weights,
-           part, part_in, mass, mass_in, centre, final,
+           part, part_in, mass, mass_in, centre, early, final,
            x_sem, own_sem, send, recv, tag_send, tag_recv, part_send, part_recv,
            fin_send, fin_recv, half_send, half_recv, out_sem):
     own, hlp = lax.axis_index("own"), lax.axis_index("help")
@@ -227,16 +227,18 @@
         swap(0, n).start()
     turn(7)
     below = divisor(0)
-    squared = jnp.zeros((SUB, 1), f32)
-    for n in range(PARTS):
-        squared = squared + combine(0, n, below)
-
-    def iteration(t, squared):
-        bias = squared * 0.125
+    squared = combine(0, 0, below)
+
+    def iteration(t, carried):
+        squared, below = carried
+        blocks = [slice(g * 8 * MOST, (g + 1) * 8 * MOST) for g in range(8)]
+        for lanes in blocks:
+            early[:, lanes] = jnp.dot(centre[:, :WIDE], turned[:WIDE, lanes], preferred_element_type=f32)
+        bias = (squared + combine(t, 1, below)) * 0.125
         heavy = jnp.zeros((SUB, 128), f32)
-        for g in range(8):
-            lanes = slice(g * 8 * MOST, (g + 1) * 8 * MOST)
-            product = jnp.dot(centre[...], turned[:, lanes], preferred_element_type=f32)
+        for lanes in blocks:
+            product = early[:, lanes] + jnp.dot(
+                centre[:, WIDE:], turned[WIDE:, lanes], preferred_element_type=f32)
             score = product * 0.25 - bias
             grown = jnp.exp(score - jnp.max(score, axis=0, keepdims=True))
             weight = (grown / jnp.sum(grown, axis=0, keepdims=True) * live[0:1, lanes]).astype(bf16)
@@ -245,28 +247,23 @@
             heavy = heavy + sum(wide[:, k * 128:(k + 1) * 128] for k in range(5))
         mass[t + 1] = heavy
         swap_mass(t + 1).start()
-
-        def finish(n, below):
-            after = combine(t + 1, n, below)
-
-            @pl.when(t == ITERS - 1)
-            def _():
-                for d in (2, 1, 3):
-                    along(d, n).start()
-            return after
-
-        squared = jnp.zeros((SUB, 1), f32)
         for n in range(PARTS):
             part[t + 1, n] = jnp.dot(weights[...], block[:, n * WIDE:(n + 1) * WIDE],
                                      preferred_element_type=f32)
             swap(t + 1, n).start()
-            if n == 0:
-                below = divisor(t + 1)
-            else:
-                squared = squared + finish(n - 1, below)
-        return squared + finish(PARTS - 1, below)
-
-    lax.fori_loop(0, ITERS, iteration, squared)
+        below = divisor(t + 1)
+        squared = combine(t + 1, 0, below)
+
+        @pl.when(t == ITERS - 1)
+        def _():
+            for d in (2, 1, 3):
+                along(d, 0).start()
+        return squared, below
+
+    squared, below = lax.fori_loop(0, ITERS, iteration, (squared, below))
+    combine(ITERS, 1, below)
+    for d in (2, 1, 3):
+        along(d, 1).start()
 
     for n in range(PARTS):
         store(0, n).start()
@@ -325,6 +322,7 @@
             pltpu.VMEM((ITERS + 1, SUB, 128), f32),
             pltpu.VMEM((ITERS + 1, SUB, 128), f32),
             pltpu.VMEM((SUB, width), bf16),
+            pltpu.VMEM((SUB, CLUSTERS * MOST), f32),
             pltpu.VMEM((CL_DEV, PARTS, SUB, WIDE), f32),
             dma, dma, dma, dma((CLUSTERS,)), dma((CLUSTERS,)), dma((CLUSTERS,)),
             dma((3 * (ITERS + 1),)), dma((3 * (ITERS + 1),)),

time: 172 us -> 171 us (level)
    pallas_call x1, Pallas kernels: 166 us -> 165 us  [shards(): pl.pallas_call(kernel, out_shape=jax.ShapeDtypeStruct((CL_DEV, SUB, width...]
where the time goes in v6:
time: 171 us; the launch traced here: 168 us
  Pallas kernels  165 us (96%)
  local copies, waits for them, and re-layouts  2.87 us (2%)
    pallas_call x1, Pallas kernels, shards(): pl.pallas_call(kernel, out_shape=jax.ShapeDtypeStruct((CL_DEV, SUB, width...  165 us

profile of v6, /device:TPU:33, one launch (start us, length us, event | category | flops | bytes accessed | tf_op | source)
XLA Modules:
  0.0 167.6 jit_solution(11891811135426791437)
XLA Ops:
  0.0 164.7 %shard_map.37 = f32[4,64,1024]{2,1,0:T(8,128)} custom-call(bf16[4096,1024]{1,0:T(8,128)(2,1)} %x_hbm.1, s32[1,4096]{1,0:T(1,128)} %bitcast.4, s32[1,4096]{1,0:T(1,128)} %bitcast.5), custom_call_target="tpu_custom_call" | custom-call | tf_op jit(solution)/shard_map/pallas_call | solution.py:303
  164.7 2.9 %copy.4 = f32[64,4,1024]{2,1,0:T(4,128)} copy(f32[64,4,1024]{2,0,1:T(8,128)} %bitcast.3) | data formatting | bytes 2097152 | tf_op jit(solution)/shard_map/transpose | solution.py:334

commit v7 on v6

--- a/solution.py
+++ b/solution.py
@@ -30,7 +30,7 @@
 
 def kernel(x_hbm, label_ref, init_ref, out_ref,
            x, packed, block, turned, pick, key, owner, tags, tags_in, live, weights,
-           part, part_in, mass, mass_in, centre, early, final,
+           part, part_in, mass, mass_in, centre, early, final, final16,
            x_sem, own_sem, send, recv, tag_send, tag_recv, part_send, part_recv,
            fin_send, fin_recv, half_send, half_recv, out_sem):
     own, hlp = lax.axis_index("own"), lax.axis_index("help")
@@ -198,29 +198,33 @@
     def combine(t, n, below):
         swap(t, n).wait_recv()
         current = (part[t, n] + part_in[t, n]) / below
-        final[cy, n] = current
-        centre[:, n * WIDE:(n + 1) * WIDE] = current.astype(bf16)
+        current16 = current.astype(bf16)
+        final16[cy, n] = current16
+        centre[:, n * WIDE:(n + 1) * WIDE] = current16
         return jnp.sum(current * current, axis=1, keepdims=True)
 
     half = pl.ds(core * 32, 32)
 
     def along(d, n):
         return pltpu.make_async_remote_copy(
-            src_ref=final.at[cy, n, half], dst_ref=final.at[cy, n, half],
+            src_ref=final16.at[cy, n, half], dst_ref=final16.at[cy, n, half],
             send_sem=fin_send.at[d * 2 + n], recv_sem=fin_recv.at[d * 2 + n],
             device_id=(own, (cy + d) % 4 * 2 + core), device_id_type=MESH)
 
     def across(d, n):
-        there = final.at[(cy + 4 - d) % 4, n, half]
+        there = final16.at[(cy + 4 - d) % 4, n, half]
         return pltpu.make_async_remote_copy(
             src_ref=there, dst_ref=there,
             send_sem=half_send.at[d * 2 + n], recv_sem=half_recv.at[d * 2 + n],
             device_id=sibling, device_id_type=MESH)
 
+    def widen(d, n):
+        final[d, n] = final16[(cy + 4 - d) % 4, n].astype(f32)
+
     def store(d, n):
         j = (cy + 4 - d) % 4
         return pltpu.make_async_copy(
-            final.at[j, n], out_ref.at[j, :, pl.ds(n * WIDE, WIDE)], out_sem.at[d * 2 + n])
+            final.at[d, n], out_ref.at[j, :, pl.ds(n * WIDE, WIDE)], out_sem.at[d * 2 + n])
 
     swap_mass(0).start()
     for n in range(PARTS):
@@ -266,6 +270,7 @@
         along(d, 1).start()
 
     for n in range(PARTS):
+        widen(0, n)
         store(0, n).start()
 
     @pl.loop(0, WINDOW - 1)
@@ -287,6 +292,7 @@
     for n in range(PARTS):
         for d in (1, 3, 2):
             across(d, n).wait_recv()
+            widen(d, n)
             store(d, n).start()
 
     for n in range(PARTS):
@@ -324,6 +330,7 @@
             pltpu.VMEM((SUB, width), bf16),
             pltpu.VMEM((SUB, CLUSTERS * MOST), f32),
             pltpu.VMEM((CL_DEV, PARTS, SUB, WIDE), f32),
+            pltpu.VMEM((CL_DEV, PARTS, SUB, WIDE), bf16),
             dma, dma, dma, dma((CLUSTERS,)), dma((CLUSTERS,)), dma((CLUSTERS,)),
             dma((3 * (ITERS + 1),)), dma((3 * (ITERS + 1),)),
             dma((8,)), dma((8,)), dma((8,)), dma((8,)), dma((8,)),

time: 171 us -> 168 us (0.982)
  Pallas kernels: 165 us -> 162 us
    pallas_call x1, Pallas kernels: 165 us -> 162 us  [shards(): pl.pallas_call(kernel, out_shape=jax.ShapeDtypeStruct((CL_DEV, SUB, width...]
where the time goes in v7:
time: 168 us; the launch traced here: 165 us
  Pallas kernels  162 us (96%)
  local copies, waits for them, and re-layouts  2.87 us (2%)
    pallas_call x1, Pallas kernels, shards(): pl.pallas_call(kernel, out_shape=jax.ShapeDtypeStruct((CL_DEV, SUB, width...  162 us

profile of v7, /device:TPU:33, one launch (start us, length us, event | category | flops | bytes accessed | tf_op | source)
XLA Modules:
  0.0 165.4 jit_solution(12457390595370971646)
XLA Ops:
  0.0 162.5 %shard_map.37 = f32[4,64,1024]{2,1,0:T(8,128)} custom-call(bf16[4096,1024]{1,0:T(8,128)(2,1)} %x_hbm.1, s32[1,4096]{1,0:T(1,128)} %bitcast.4, s32[1,4096]{1,0:T(1,128)} %bitcast.5), custom_call_target="tpu_custom_call" | custom-call | tf_op jit(solution)/shard_map/pallas_call | solution.py:309
  162.5 2.9 %copy.4 = f32[64,4,1024]{2,1,0:T(4,128)} copy(f32[64,4,1024]{2,0,1:T(8,128)} %bitcast.3) | data formatting | bytes 2097152 | tf_op jit(solution)/shard_map/transpose | solution.py:341
